TPU v7x, 32 devices: a whole 2x2x4 slice. The times are simulated.
32 devices in a mesh: region: 8 (over y, x, core), tile: 4 (over z).
Axes of the slice: x: 2, y: 2, z: 4, core: 2. Of those that a mesh axis runs over, the one named last changes fastest.
Arguments:
- state: float32 [80, 4, 16384], P(None, 'tile', 'region'), may hold values from -6 to 6
- obs_rows: float32 [8, 80, 4, 128], P('region', None, 'tile'), may hold values from -6 to 6
- obs_value: float32 [8, 4, 128], P('region', 'tile'), may hold values from -6 to 6
- obs_noise: float32 [8, 4, 128], P('region', 'tile'), may hold values from 0.3 to 3
- obs_cell: int32 [8, 4, 128], P('region', 'tile'), may hold values from 0 to 16383
- obs_class: int32 [8, 4, 128], P('region', 'tile'), may hold values from 0 to 2
- obs_count: int32 [8, 4], P('region', 'tile'), may hold values from 1 to 128, 256 in all within a row
Outputs:
- posterior: float32 [80, 4, 16384], P(None, 'tile', 'region')
Inputs may be any that keep to these rules, and one draw needn't show every extreme that they name: `obs_count`: in every batch some tile has exactly 128 live slots.
All inputs are finite; a program needn't handle non-finite values. No bound on the sum of `obs_count` on one device may be relied on, other than what follows from the above.
Results may differ from a plain program's by a relative error of at most 0.0003.
Values sent between devices are 32-bit elements; how exact they have to be, the bound alone decides.
A program may use at most 64 MiB of HBM per device.

v0:
```python
import functools

import jax
import jax.numpy as jnp
from jax import lax
from jax.experimental import pallas as pl
from jax.experimental.pallas import tpu as pltpu
from jax.sharding import PartitionSpec as P

EPSILON = 1e-06
LANES = 256
GROUP = 2
F32 = jnp.float32
BF16 = jnp.bfloat16


def split(x):
    high = x.astype(BF16)
    return high, (x - high.astype(F32)).astype(BF16)


def kernel(nbatch, tiles, members, width, scal_ref, obs_ref, state_ref, out_ref,
           z_ref, pos_ref, info_ref, lhs_ref, inc_ref, pk_ref, wk_ref):
    slots = obs_ref.shape[2]
    rows = obs_ref.shape[1]
    cells = state_ref.shape[1]
    first = nbatch * width
    total = first + cells
    depth = lhs_ref.shape[1]
    pad = depth - 3 * members
    lane = lax.broadcasted_iota(jnp.int32, (1, width), 1)

    def compact(b, carry):
        acc = jnp.zeros((rows, width), F32)
        start = jnp.int32(0)
        for t in range(tiles):
            count = scal_ref[b * tiles + t]
            x = obs_ref[b * tiles + t]
            x = jnp.concatenate([x, jnp.zeros((rows, width - slots), F32)], axis=1)
            x = pltpu.roll(x, start, 1)
            here = (lane >= start) & (lane < start + count)
            acc = jnp.where(here, x, acc)
            start = start + count
        cols = pl.ds(pl.multiple_of(b * width, width), width)
        z_ref[:, cols] = acc[:members]
        info_ref[b] = acc[members:]
        pos_ref[:, cols] = jnp.broadcast_to(acc[members + 2 : members + 3], (8, width))
        return carry

    lax.fori_loop(0, nbatch, compact, 0)
    z_ref[:, first:] = state_ref[...]
    cell = scal_ref[nbatch * tiles] + lax.broadcasted_iota(jnp.int32, (8, cells), 1)
    pos_ref[:, first:] = cell.astype(F32)

    def step(b, carry):
        cols = pl.ds(pl.multiple_of(b * width, width), width)
        now = z_ref[:, cols]
        info = info_ref[b]
        value, noise = info[0:1], info[1:2]
        mean = jnp.sum(now, axis=0, keepdims=True) / members
        anomaly = now - mean
        prior = jnp.sum(anomaly * anomaly, axis=0, keepdims=True) / (members - 1) + EPSILON
        post = 1.0 / (1.0 / prior + 1.0 / noise)
        shift = post * (mean / prior + value / noise) - mean
        factor = jnp.sqrt(post / prior) - 1.0
        increment = shift + factor * anomaly
        inc_high, inc_low = split(increment)
        inc_ref[...] = jnp.concatenate([inc_high, inc_low], axis=0)
        scaled = anomaly * (1.0 / ((members - 1) * prior))
        high = scaled.astype(BF16).astype(F32)
        stacked = jnp.concatenate(
            [high, high, scaled - high, jnp.zeros((pad, width), F32)], axis=0
        )
        lhs_ref[...] = jnp.transpose(stacked).astype(BF16)
        turned = jnp.transpose(jnp.concatenate([info] * 16, axis=0))
        pk_ref[...] = jnp.broadcast_to(turned[:, 2:3], (width, LANES))
        wk_ref[...] = jnp.broadcast_to(turned[:, 3:4], (width, LANES))

        def group(g, inner):
            base = g * (GROUP * LANES)
            spans = [
                pl.ds(pl.multiple_of(base + i * LANES, LANES), LANES) for i in range(GROUP)
            ]
            values = [z_ref[:, span] for span in spans]
            places = [pos_ref[0:1, span] for span in spans]
            lhs = lhs_ref[...]
            inc = inc_ref[...]
            results = []
            for z, place in zip(values, places):
                centered = z - jnp.sum(z, axis=0, keepdims=True) / members
                z_high, z_low = split(centered)
                rhs = jnp.concatenate(
                    [z_high, z_low, z_high, jnp.zeros((pad, LANES), BF16)], axis=0
                )
                cov = jnp.dot(lhs, rhs, preferred_element_type=F32)
                near = jnp.maximum(1.0 - jnp.abs(place - pk_ref[...]) * wk_ref[...], 0.0)
                gain_high, gain_low = split(near * near * cov)
                both = jnp.dot(inc, gain_high, preferred_element_type=F32)
                low = jnp.dot(inc[:members], gain_low, preferred_element_type=F32)
                results.append(z + (both[:members] + (both[members:] + low)))
            for span, result in zip(spans, results):
                z_ref[:, span] = result
            return inner

        lax.fori_loop(((b + 1) * width) // (GROUP * LANES), total // (GROUP * LANES), group, 0)
        return carry

    lax.fori_loop(0, nbatch, step, 0)
    out_ref[...] = z_ref[:, first:]


def on_device(state, obs_rows, obs_value, obs_noise, obs_cell, obs_class, obs_count):
    members = state.shape[0]
    cells = state.shape[2]
    slots = obs_rows.shape[3]
    nbatch = lax.axis_size("region")
    tiles = lax.axis_size("tile")
    region_index = lax.axis_index("region")
    tile_index = lax.axis_index("tile")
    tile_width = cells * nbatch
    width = tiles * slots // 2
    depth = -(-3 * members // 128) * 128
    own_pos = (tile_index * tile_width + obs_cell[0]).astype(F32)
    own_inv = 4.0 / (tile_width * (obs_class[0] + 2).astype(F32))
    count_row = jnp.broadcast_to(obs_count.astype(F32), (1, slots))
    packed = jnp.concatenate(
        [obs_rows[0, :, 0, :], obs_value[0], obs_noise[0], own_pos, own_inv, count_row,
         jnp.zeros((3, slots), F32)], axis=0
    )
    rows = packed.shape[0]
    gathered = lax.all_gather(packed, ("region", "tile"), axis=0)
    counts = gathered[:, members + 4, 0].astype(jnp.int32)
    base = (tile_index * tile_width + region_index * cells).astype(jnp.int32)
    scalars = jnp.concatenate([counts, base[None]])
    total = nbatch * width + cells
    vmem = pl.BlockSpec(memory_space=pltpu.VMEM)
    out = pl.pallas_call(
        functools.partial(kernel, nbatch, tiles, members, width),
        out_shape=jax.ShapeDtypeStruct((members, cells), F32),
        in_specs=[pl.BlockSpec(memory_space=pltpu.SMEM), vmem, vmem],
        out_specs=vmem,
        scratch_shapes=[
            pltpu.VMEM((members, total), F32),
            pltpu.VMEM((8, total), F32),
            pltpu.VMEM((nbatch, rows - members, width), F32),
            pltpu.VMEM((width, depth), BF16),
            pltpu.VMEM((2 * members, width), BF16),
            pltpu.VMEM((width, LANES), F32),
            pltpu.VMEM((width, LANES), F32),
        ],
        compiler_params=pltpu.CompilerParams(vmem_limit_bytes=40 * 1024 * 1024),
    )(scalars, gathered, state[:, 0, :])
    return out[:, None, :]


def solution(mesh):
    placed = (
        P(None, "tile", "region"),
        P("region", None, "tile", None),
        P("region", "tile", None),
        P("region", "tile", None),
        P("region", "tile", None),
        P("region", "tile", None),
        P("region", "tile"),
    )
    return jax.shard_map(
        on_device, mesh=mesh, in_specs=placed, out_specs=P(None, "tile", "region"), check_vma=False
    )
```

profile of v0, /device:TPU:0, one launch (start us, length us, event | category | flops | bytes accessed | tf_op | source)
XLA Modules:
  0.0 107.5 jit_solution(11359665259502018595)
XLA Ops:
  6.5 0.0 all-gather.3.cloned.1.call-start
  7.2 0.7 divide_bitcast_fusion
  7.9 0.7 convert_bitcast_fusion
  8.5 2.7 %concatenate.6 = f32[88,128]{1,0:T(8,128)} concatenate(f32[80,128]{1,0:T(8,128)} %bitcast.18, f32[1,128]{1,0:T(1,128)} %bitcast.19, f32[1,128]{1,0:T(1,128)} %bitcast.20, f32[1,128]{1,0:T(1,128)S(1)} %convert_bitcast_fusion, f32[1,128]{1,0:T(1,128)S(1)} %divide_bitcast_fusion, f32[1,128]{1,0:T(1,128)S(1)} %broadcast_in_dim.17, f32[3,128]{1,0:T(4,128)S(1)} %broadcast_in_dim.18), dimensions={0} | concatenate | bytes 90112 | tf_op jit(solution)/shard_map/concatenate | solution.py:126
  11.2 0.0 all-gather.3.cloned.1.call-update
  11.2 1.3 %copy.12 = f32[80,1,2048]{2,0,1:T(8,128)S(1)} copy(f32[80,1,2048]{2,1,0:T(1,128)} %param.7) | data formatting | bytes 1310720
  12.5 56.3 %all-gather.3.cloned.1.call-done = f32[2816,128]{1,0:T(8,128)} async-done(((f32[88,128]{1,0:T(8,128)}), f32[2816,128]{1,0:T(8,128)}) %all-gather.3.cloned.1.call-update) | async-done | bytes 1441808 | tf_op jit(solution)/shard_map/all_gather | solution.py:131
  68.9 1.6 %fusion = s32[32]{0:T(128)S(1)} fusion(f32[32,88,128]{2,1,0:T(8,128)} %bitcast.16), kind=kLoop, calls=%fused_computation.2 | loop fusion | flops 32 | bytes 256 | tf_op jit(solution)/shard_map/convert_element_type | solution.py:132
  70.4 0.1 pad_add_fusion.scal_ref
  70.5 0.0 copy-start
  70.5 1.4 %copy-done = f32[2816,128]{1,0:T(8,128)S(1)} copy-done((f32[2816,128]{1,0:T(8,128)S(1)}, f32[2816,128]{1,0:T(8,128)}, u32[]{:S(2)}) %copy-start) | copy-done | bytes 1441816
  71.9 27.3 %shard_map.73 = f32[80,2048]{1,0:T(8,128)S(1)} custom-call(s32[33]{0:T(128)S(1)} %pad_add_fusion.scal_ref, f32[32,88,128]{2,1,0:T(8,128)S(1)} %bitcast.17, f32[80,2048]{1,0:T(8,128)S(1)} %bitcast.14), custom_call_target="tpu_custom_call" | custom-call | tf_op jit(solution)/shard_map/pallas_call | solution.py:137
  99.2 1.5 %copy.9 = f32[80,1,2048]{2,1,0:T(1,128)} copy(f32[80,1,2048]{2,0,1:T(8,128)S(1)} %bitcast.15) | data formatting | bytes 1310720 | tf_op jit(solution)/shard_map/broadcast_in_dim | solution.py:153
  (2 shorter events, 0.0 us)
Async XLA Ops:
  6.5 62.3 %all-gather.3.cloned.1.call-start = ((), (), s32[]{:S(2)}) async-start(), calls=%async_computation | async-start | bytes 1486848 | tf_op jit(solution)/shard_map/all_gather | solution.py:131
  70.5 1.4 %copy-start = (f32[2816,128]{1,0:T(8,128)S(1)}, f32[2816,128]{1,0:T(8,128)}, u32[]{:S(2)}) copy-start(f32[2816,128]{1,0:T(8,128)} %all-gather.3.cloned.1.call-done) | copy-start | bytes 4325380
Sparse Core Ops, SparseCore 0:
  11.3 57.4 all-gather.2
where the time goes:
time: 108 us
  waiting for transfers between devices  56.4 us (52%)
  Pallas kernels  27.3 us (25%)
  between operations  14.1 us (13%)
  local copies, waits for them, and re-layouts  6.85 us (6%)
  other arithmetic  2.97 us (3%)
    all_gather x1, waiting for transfers between devices, on_device(): gathered = lax.all_gather(packed, ('region', 'tile'), axis=0)  56.3 us
    pallas_call x1, Pallas kernels, on_device(): pl.pallas_call(functools.partial(kernel, nbatch, tiles, members, width),...  27.3 us
    concatenate x1, local copies, waits for them, and re-layouts, on_device(): jnp.concatenate([obs_rows[0, :, 0, :], obs_value[0], obs_noise[0], own_po...  2.67 us
    unnamed x3, local copies, waits for them, and re-layouts  2.67 us
  transfers between devices with their start and end apart: 1, of which 1 were waited for; matrix products, arithmetic and copies ran while one was open for 1% of the time, Pallas kernels for 0%

commit v1 on v0

--- a/solution.py
+++ b/solution.py
@@ -19,37 +19,92 @@
     return high, (x - high.astype(F32)).astype(BF16)
 
 
-def kernel(nbatch, tiles, members, width, scal_ref, obs_ref, state_ref, out_ref,
+def gather_kernel(nbatch, tiles, members, width, tile_width, count_ref, rows_ref, value_ref,
+                  noise_ref, cell_ref, class_ref, out_ref, own_ref, slab_ref, live_ref,
+                  tile_send, tile_recv, region_send, region_recv, local_sem):
+    region = lax.axis_index("region")
+    tile = lax.axis_index("tile")
+    slots = rows_ref.shape[1]
+    barrier = pltpu.get_barrier_semaphore()
+    for i in range(1, tiles):
+        pl.semaphore_signal(barrier, inc=1, device_id=(region, lax.rem(tile + i, tiles)),
+                            device_id_type=pl.DeviceIdType.MESH)
+    for i in range(1, nbatch):
+        pl.semaphore_signal(barrier, inc=1, device_id=(lax.rem(region + i, nbatch), tile),
+                            device_id_type=pl.DeviceIdType.MESH)
+
+    spot = (tile * tile_width + cell_ref[...]).astype(F32)
+    inv = 4.0 / (tile_width * (class_ref[...] + 2).astype(F32))
+    count = jnp.full((1, slots), count_ref[0, 0], jnp.int32).astype(F32)
+    own_ref[0:members] = rows_ref[...]
+    own_ref[members:] = jnp.concatenate(
+        [value_ref[...], noise_ref[...], spot, inv, count, jnp.zeros((own_ref.shape[0] - members - 5, slots), F32)], axis=0
+    )
+    pl.semaphore_wait(barrier, tiles + nbatch - 2)
+
+    copies = []
+    for i in range(1, tiles):
+        copy = pltpu.make_async_remote_copy(
+            src_ref=own_ref, dst_ref=slab_ref.at[tile],
+            send_sem=tile_send.at[i], recv_sem=tile_recv.at[i],
+            device_id=(region, lax.rem(tile + i, tiles)),
+            device_id_type=pl.DeviceIdType.MESH)
+        copy.start()
+        copies.append(copy)
+    slab_ref[tile] = own_ref[...]
+    for copy in copies:
+        copy.wait()
+
+    lane = lax.broadcasted_iota(jnp.int32, (1, slots), 1).astype(F32)
+    row = lax.broadcasted_iota(jnp.int32, (width, slots), 0).astype(F32)
+    start = jnp.zeros((1, slots), F32)
+    picks, parts = [], []
+    for t in range(tiles):
+        block = slab_ref[t]
+        count = block[members + 4 : members + 5]
+        place = jnp.where(lane < count, start + lane, -1.0)
+        picks.append(jnp.where(row == place, 1.0, 0.0).astype(BF16))
+        start = start + count
+        high = block.astype(BF16)
+        rest = block - high.astype(F32)
+        middle, low = split(rest)
+        parts.append(jnp.concatenate([high, middle, low], axis=0))
+    moved = lax.dot_general(
+        jnp.concatenate(parts, axis=1), jnp.concatenate(picks, axis=1),
+        (((1,), (1,)), ((), ())), preferred_element_type=F32)
+    count_rows = own_ref.shape[0]
+    live_ref[...] = moved[:count_rows] + (
+        moved[count_rows : 2 * count_rows] + moved[2 * count_rows : 3 * count_rows])
+
+    copies = [pltpu.make_async_copy(live_ref, out_ref.at[region], local_sem)]
+    for i in range(1, nbatch):
+        copies.append(pltpu.make_async_remote_copy(
+            src_ref=live_ref, dst_ref=out_ref.at[region],
+            send_sem=region_send.at[i], recv_sem=region_recv.at[i],
+            device_id=(lax.rem(region + i, nbatch), tile),
+            device_id_type=pl.DeviceIdType.MESH))
+    for copy in copies[1:] + copies[:1]:
+        copy.start()
+    for copy in copies:
+        copy.wait()
+
+
+def kernel(nbatch, members, width, scal_ref, obs_ref, state_ref, out_ref,
            z_ref, pos_ref, info_ref, lhs_ref, inc_ref, pk_ref, wk_ref):
-    slots = obs_ref.shape[2]
-    rows = obs_ref.shape[1]
     cells = state_ref.shape[1]
     first = nbatch * width
     total = first + cells
     depth = lhs_ref.shape[1]
     pad = depth - 3 * members
-    lane = lax.broadcasted_iota(jnp.int32, (1, width), 1)
-
-    def compact(b, carry):
-        acc = jnp.zeros((rows, width), F32)
-        start = jnp.int32(0)
-        for t in range(tiles):
-            count = scal_ref[b * tiles + t]
-            x = obs_ref[b * tiles + t]
-            x = jnp.concatenate([x, jnp.zeros((rows, width - slots), F32)], axis=1)
-            x = pltpu.roll(x, start, 1)
-            here = (lane >= start) & (lane < start + count)
-            acc = jnp.where(here, x, acc)
-            start = start + count
-        cols = pl.ds(pl.multiple_of(b * width, width), width)
-        z_ref[:, cols] = acc[:members]
-        info_ref[b] = acc[members:]
-        pos_ref[:, cols] = jnp.broadcast_to(acc[members + 2 : members + 3], (8, width))
-        return carry
-
-    lax.fori_loop(0, nbatch, compact, 0)
+
+    for b in range(nbatch):
+        cols = pl.ds(b * width, width)
+        block = obs_ref[b]
+        z_ref[:, cols] = block[:members]
+        info_ref[b] = block[members:]
+        pos_ref[:, cols] = jnp.broadcast_to(block[members + 2 : members + 3], (8, width))
     z_ref[:, first:] = state_ref[...]
-    cell = scal_ref[nbatch * tiles] + lax.broadcasted_iota(jnp.int32, (8, cells), 1)
+    cell = scal_ref[0] + lax.broadcasted_iota(jnp.int32, (8, cells), 1)
     pos_ref[:, first:] = cell.astype(F32)
 
     def step(b, carry):
@@ -72,7 +127,7 @@
             [high, high, scaled - high, jnp.zeros((pad, width), F32)], axis=0
         )
         lhs_ref[...] = jnp.transpose(stacked).astype(BF16)
-        turned = jnp.transpose(jnp.concatenate([info] * 16, axis=0))
+        turned = jnp.transpose(jnp.concatenate([info] * (128 // info.shape[0]), axis=0))
         pk_ref[...] = jnp.broadcast_to(turned[:, 2:3], (width, LANES))
         wk_ref[...] = jnp.broadcast_to(turned[:, 3:4], (width, LANES))
 
@@ -120,24 +175,33 @@
     tile_width = cells * nbatch
     width = tiles * slots // 2
     depth = -(-3 * members // 128) * 128
-    own_pos = (tile_index * tile_width + obs_cell[0]).astype(F32)
-    own_inv = 4.0 / (tile_width * (obs_class[0] + 2).astype(F32))
-    count_row = jnp.broadcast_to(obs_count.astype(F32), (1, slots))
-    packed = jnp.concatenate(
-        [obs_rows[0, :, 0, :], obs_value[0], obs_noise[0], own_pos, own_inv, count_row,
-         jnp.zeros((3, slots), F32)], axis=0
-    )
-    rows = packed.shape[0]
-    gathered = lax.all_gather(packed, ("region", "tile"), axis=0)
-    counts = gathered[:, members + 4, 0].astype(jnp.int32)
-    base = (tile_index * tile_width + region_index * cells).astype(jnp.int32)
-    scalars = jnp.concatenate([counts, base[None]])
+    rows = -(-(members + 5) // 16) * 16
+    vmem = pl.BlockSpec(memory_space=pltpu.VMEM)
+    smem = pl.BlockSpec(memory_space=pltpu.SMEM)
+    gathered = pl.pallas_call(
+        functools.partial(gather_kernel, nbatch, tiles, members, width, tile_width),
+        out_shape=jax.ShapeDtypeStruct((nbatch, rows, width), F32),
+        in_specs=[smem] + [vmem] * 5,
+        out_specs=pl.BlockSpec(memory_space=pl.ANY),
+        scratch_shapes=[
+            pltpu.VMEM((rows, slots), F32),
+            pltpu.VMEM((tiles, rows, slots), F32),
+            pltpu.VMEM((rows, width), F32),
+            pltpu.SemaphoreType.DMA((tiles,)),
+            pltpu.SemaphoreType.DMA((tiles,)),
+            pltpu.SemaphoreType.DMA((nbatch,)),
+            pltpu.SemaphoreType.DMA((nbatch,)),
+            pltpu.SemaphoreType.DMA,
+        ],
+        compiler_params=pltpu.CompilerParams(
+            collective_id=0, has_side_effects=True, vmem_limit_bytes=24 * 1024 * 1024),
+    )(obs_count, obs_rows[0, :, 0, :], obs_value[0], obs_noise[0], obs_cell[0], obs_class[0])
+    scalars = (tile_index * tile_width + region_index * cells).astype(jnp.int32)[None]
     total = nbatch * width + cells
-    vmem = pl.BlockSpec(memory_space=pltpu.VMEM)
     out = pl.pallas_call(
-        functools.partial(kernel, nbatch, tiles, members, width),
+        functools.partial(kernel, nbatch, members, width),
         out_shape=jax.ShapeDtypeStruct((members, cells), F32),
-        in_specs=[pl.BlockSpec(memory_space=pltpu.SMEM), vmem, vmem],
+        in_specs=[smem, vmem, vmem],
         out_specs=vmem,
         scratch_shapes=[
             pltpu.VMEM((members, total), F32),

time: 108 us -> 49.5 us (0.46)
  waiting for transfers between devices: 56.4 us -> 0 us
  Pallas kernels: 27.3 us -> 44.3 us
  between operations: 14.1 us -> 0.73 us
  local copies, waits for them, and re-layouts: 6.85 us -> 3.47 us
  other arithmetic: 2.97 us -> 0 us
    all_gather x1 -> x0, waiting for transfers between devices: 56.3 us -> none  [on_device(): gathered = lax.all_gather(packed, ('region', 'tile'), axis=0)]
    pallas_call x1 -> x2, Pallas kernels: 27.3 us -> 44.3 us  [the longest x1 25.9 us: on_device(): pl.pallas_call(functools.partial(kernel, nbatch, members, width), out_sha...]
    concatenate x1 -> x0, local copies, waits for them, and re-layouts: 2.67 us -> none  [on_device(): jnp.concatenate([obs_rows[0, :, 0, :], obs_value[0], obs_noise[0], own_po...]
    convert_element_type x2 -> x0, other arithmetic: 2.23 us -> none  [the longest x1 1.56 us: on_device(): counts = gathered[:, members + 4, 0].astype(jnp.int32)]
    unnamed x3 -> x11, local copies, waits for them, and re-layouts: 2.67 us -> 1.96 us
  transfers between devices with their start and end apart: 1 -> 0, of which waited for: 1 -> 0; matrix products, arithmetic and copies ran while one was open for 1% -> 0% of each run, Pallas kernels for 0% -> 0%
where the time goes in v1:
time: 49.5 us; the launch traced here: 48.5 us
  Pallas kernels  44.3 us (89%)
  local copies, waits for them, and re-layouts  3.47 us (7%)
  between operations  0.73 us (1%)
    pallas_call x1, Pallas kernels, on_device(): pl.pallas_call(functools.partial(kernel, nbatch, members, width), out_sha...  25.9 us
    pallas_call x1, Pallas kernels, on_device(): pl.pallas_call(functools.partial(gather_kernel, nbatch, tiles, members, w...  18.4 us
    unnamed x11, local copies, waits for them, and re-layouts  1.96 us
    broadcast_in_dim x1, local copies, waits for them, and re-layouts, on_device(): return out[:, None, :]  1.51 us

profile of v1, /device:TPU:0, one launch (start us, length us, event | category | flops | bytes accessed | tf_op | source)
XLA Modules:
  0.0 48.5 jit_solution(17270671808372484734)
XLA Ops:
  0.7 0.0 copy-start
  0.7 0.0 copy-start.4
  0.7 1.3 %copy.11 = f32[80,1,2048]{2,0,1:T(8,128)S(1)} copy(f32[80,1,2048]{2,1,0:T(1,128)} %param.7) | data formatting | bytes 1310720
  2.0 0.0 copy-start.1
  2.0 0.0 copy-start.2
  2.0 0.0 copy-start.3
  2.0 0.0 copy-done
  2.0 0.0 copy-done.4
  2.0 0.6 %copy-done.1 = f32[1,1,128]{2,1,0:T(1,128)S(1)} copy-done((f32[1,1,128]{2,1,0:T(1,128)S(1)}, f32[1,1,128]{2,1,0:T(1,128)}, u32[]{:S(2)}) %copy-start.1) | copy-done | bytes 536
  2.6 0.0 copy-done.2
  2.7 0.0 copy-done.3
  2.7 18.4 %shard_map.73.obs_ref = f32[8,96,256]{2,1,0:T(8,128)S(1)} custom-call(s32[1,1]{1,0:T(1,128)S(6)} %copy.12.count_ref, f32[80,128]{1,0:T(8,128)S(1)} %bitcast.12, f32[1,128]{1,0:T(1,128)S(1)} %bitcast.13, f32[1,128]{1,0:T(1,128)S(1)} %bitcast.14, s32[1,128]{1,0:T(1,128)S(1)} %bitcast.15, s32[1,128]{1,0:T(1,128)S(1)} %bitcast.16), custom_call_target="tpu_custom_call" | custom-call | tf_op jit(solution)/shard_map/pallas_call | solution.py:181
  21.0 25.9 %shard_map.74 = f32[80,2048]{1,0:T(8,128)S(1)} custom-call(s32[1]{0:T(128)} %bitcast.scal_ref, f32[8,96,256]{2,1,0:T(8,128)S(1)} %shard_map.73.obs_ref, f32[80,2048]{1,0:T(8,128)S(1)} %bitcast.10), custom_call_target="tpu_custom_call" | custom-call | tf_op jit(solution)/shard_map/pallas_call | solution.py:201
  47.0 1.5 %copy.8 = f32[80,1,2048]{2,1,0:T(1,128)} copy(f32[80,1,2048]{2,0,1:T(8,128)S(1)} %bitcast.11) | data formatting | bytes 1310720 | tf_op jit(solution)/shard_map/broadcast_in_dim | solution.py:217
Async XLA Ops:
  0.7 1.4 %copy-start = (f32[1,80,1,128]{3,2,1,0:T(1,128)S(1)}, f32[1,80,1,128]{3,2,1,0:T(1,128)}, u32[]{:S(2)}) copy-start(f32[1,80,1,128]{3,2,1,0:T(1,128)} %param.8) | copy-start | bytes 122884
  0.7 1.4 %copy-start.4 = (s32[1,1,128]{2,1,0:T(1,128)S(1)}, s32[1,1,128]{2,1,0:T(1,128)}, u32[]{:S(2)}) copy-start(s32[1,1,128]{2,1,0:T(1,128)} %param.12) | copy-start | bytes 1540
  2.0 0.7 %copy-start.1 = (f32[1,1,128]{2,1,0:T(1,128)S(1)}, f32[1,1,128]{2,1,0:T(1,128)}, u32[]{:S(2)}) copy-start(f32[1,1,128]{2,1,0:T(1,128)} %param.9) | copy-start | bytes 1540
  2.0 0.7 %copy-start.2 = (f32[1,1,128]{2,1,0:T(1,128)S(1)}, f32[1,1,128]{2,1,0:T(1,128)}, u32[]{:S(2)}) copy-start(f32[1,1,128]{2,1,0:T(1,128)} %param.10) | copy-start | bytes 1540
  2.0 0.7 %copy-start.3 = (s32[1,1,128]{2,1,0:T(1,128)S(1)}, s32[1,1,128]{2,1,0:T(1,128)}, u32[]{:S(2)}) copy-start(s32[1,1,128]{2,1,0:T(1,128)} %param.11) | copy-start | bytes 1540

commit v2 on v1

--- a/solution.py
+++ b/solution.py
@@ -10,6 +10,7 @@
 EPSILON = 1e-06
 LANES = 256
 GROUP = 2
+CELL_GROUP = 4
 F32 = jnp.float32
 BF16 = jnp.bfloat16
 
@@ -21,7 +22,8 @@
 
 def gather_kernel(nbatch, tiles, members, width, tile_width, count_ref, rows_ref, value_ref,
                   noise_ref, cell_ref, class_ref, out_ref, own_ref, slab_ref, live_ref,
-                  tile_send, tile_recv, region_send, region_recv, local_sem):
+                  tile_send, tile_recv, region_send, region_recv, pass_send, pass_recv,
+                  local_sem):
     region = lax.axis_index("region")
     tile = lax.axis_index("tile")
     slots = rows_ref.shape[1]
@@ -29,8 +31,11 @@
     for i in range(1, tiles):
         pl.semaphore_signal(barrier, inc=1, device_id=(region, lax.rem(tile + i, tiles)),
                             device_id_type=pl.DeviceIdType.MESH)
-    for i in range(1, nbatch):
-        pl.semaphore_signal(barrier, inc=1, device_id=(lax.rem(region + i, nbatch), tile),
+    pairs = nbatch // 2
+    sibling = region + 1 - 2 * lax.rem(region, 2)
+    for i in range(pairs):
+        peer = lax.rem(region + 2 * i, nbatch) if i else sibling
+        pl.semaphore_signal(barrier, inc=1, device_id=(peer, tile),
                             device_id_type=pl.DeviceIdType.MESH)
 
     spot = (tile * tile_width + cell_ref[...]).astype(F32)
@@ -40,7 +45,7 @@
     own_ref[members:] = jnp.concatenate(
         [value_ref[...], noise_ref[...], spot, inv, count, jnp.zeros((own_ref.shape[0] - members - 5, slots), F32)], axis=0
     )
-    pl.semaphore_wait(barrier, tiles + nbatch - 2)
+    pl.semaphore_wait(barrier, tiles + pairs - 1)
 
     copies = []
     for i in range(1, tiles):
@@ -59,33 +64,46 @@
     row = lax.broadcasted_iota(jnp.int32, (width, slots), 0).astype(F32)
     start = jnp.zeros((1, slots), F32)
     picks, parts = [], []
+    fill = -3 * own_ref.shape[0] % 16
     for t in range(tiles):
         block = slab_ref[t]
         count = block[members + 4 : members + 5]
         place = jnp.where(lane < count, start + lane, -1.0)
         picks.append(jnp.where(row == place, 1.0, 0.0).astype(BF16))
         start = start + count
-        high = block.astype(BF16)
-        rest = block - high.astype(F32)
-        middle, low = split(rest)
-        parts.append(jnp.concatenate([high, middle, low], axis=0))
+        high = block.astype(BF16).astype(F32)
+        middle = (block - high).astype(BF16).astype(F32)
+        low = block - high - middle
+        parts.append(jnp.concatenate([high, middle, low, jnp.zeros((fill, slots), F32)], axis=0))
     moved = lax.dot_general(
-        jnp.concatenate(parts, axis=1), jnp.concatenate(picks, axis=1),
+        jnp.concatenate(parts, axis=1).astype(BF16), jnp.concatenate(picks, axis=1),
         (((1,), (1,)), ((), ())), preferred_element_type=F32)
     count_rows = own_ref.shape[0]
     live_ref[...] = moved[:count_rows] + (
         moved[count_rows : 2 * count_rows] + moved[2 * count_rows : 3 * count_rows])
 
-    copies = [pltpu.make_async_copy(live_ref, out_ref.at[region], local_sem)]
-    for i in range(1, nbatch):
-        copies.append(pltpu.make_async_remote_copy(
-            src_ref=live_ref, dst_ref=out_ref.at[region],
-            send_sem=region_send.at[i], recv_sem=region_recv.at[i],
-            device_id=(lax.rem(region + i, nbatch), tile),
-            device_id_type=pl.DeviceIdType.MESH))
-    for copy in copies[1:] + copies[:1]:
+    def send(src, block, peer, send_sem, recv_sem):
+        copy = pltpu.make_async_remote_copy(
+            src_ref=src, dst_ref=out_ref.at[block], send_sem=send_sem, recv_sem=recv_sem,
+            device_id=(peer, tile), device_id_type=pl.DeviceIdType.MESH)
         copy.start()
-    for copy in copies:
+        return copy
+
+    across = [
+        send(live_ref, region, lax.rem(region + 2 * i, nbatch), region_send.at[i], region_recv.at[i])
+        for i in range(1, pairs)
+    ]
+    passed = [send(live_ref, region, sibling, pass_send.at[0], pass_recv.at[0])]
+    local = pltpu.make_async_copy(live_ref, out_ref.at[region], local_sem)
+    local.start()
+    for i in range(1, pairs):
+        across[i - 1].wait_recv()
+        block = lax.rem(region + nbatch - 2 * i, nbatch)
+        passed.append(send(out_ref.at[block], block, sibling, pass_send.at[i], pass_recv.at[i]))
+    local.wait()
+    for copy in across:
+        copy.wait_send()
+    for copy in passed:
         copy.wait()
 
 
@@ -131,10 +149,10 @@
         pk_ref[...] = jnp.broadcast_to(turned[:, 2:3], (width, LANES))
         wk_ref[...] = jnp.broadcast_to(turned[:, 3:4], (width, LANES))
 
-        def group(g, inner):
-            base = g * (GROUP * LANES)
+        def group(size, offset, g, inner):
+            base = offset + g * (size * LANES)
             spans = [
-                pl.ds(pl.multiple_of(base + i * LANES, LANES), LANES) for i in range(GROUP)
+                pl.ds(pl.multiple_of(base + i * LANES, LANES), LANES) for i in range(size)
             ]
             values = [z_ref[:, span] for span in spans]
             places = [pos_ref[0:1, span] for span in spans]
@@ -157,7 +175,11 @@
                 z_ref[:, span] = result
             return inner
 
-        lax.fori_loop(((b + 1) * width) // (GROUP * LANES), total // (GROUP * LANES), group, 0)
+        near_count = GROUP * LANES
+        lax.fori_loop(((b + 1) * width) // near_count, first // near_count,
+                      functools.partial(group, GROUP, 0), 0)
+        lax.fori_loop(0, cells // (CELL_GROUP * LANES),
+                      functools.partial(group, CELL_GROUP, first), 0)
         return carry
 
     lax.fori_loop(0, nbatch, step, 0)
@@ -175,7 +197,7 @@
     tile_width = cells * nbatch
     width = tiles * slots // 2
     depth = -(-3 * members // 128) * 128
-    rows = -(-(members + 5) // 16) * 16
+    rows = -(-(members + 5) // 8) * 8
     vmem = pl.BlockSpec(memory_space=pltpu.VMEM)
     smem = pl.BlockSpec(memory_space=pltpu.SMEM)
     gathered = pl.pallas_call(
@@ -189,8 +211,10 @@
             pltpu.VMEM((rows, width), F32),
             pltpu.SemaphoreType.DMA((tiles,)),
             pltpu.SemaphoreType.DMA((tiles,)),
-            pltpu.SemaphoreType.DMA((nbatch,)),
-            pltpu.SemaphoreType.DMA((nbatch,)),
+            pltpu.SemaphoreType.DMA((nbatch // 2,)),
+            pltpu.SemaphoreType.DMA((nbatch // 2,)),
+            pltpu.SemaphoreType.DMA((nbatch // 2,)),
+            pltpu.SemaphoreType.DMA((nbatch // 2,)),
             pltpu.SemaphoreType.DMA,
         ],
         compiler_params=pltpu.CompilerParams(

time: 49.5 us -> 41.3 us (0.83); the launches traced: 48.5 us -> 41.1 us
  Pallas kernels: 44.3 us -> 36.9 us
    pallas_call x1, Pallas kernels: 25.9 us -> 20.6 us  [on_device(): pl.pallas_call(functools.partial(kernel, nbatch, members, width), out_sha...]
    pallas_call x1, Pallas kernels: 18.4 us -> 16.4 us  [on_device(): pl.pallas_call(functools.partial(gather_kernel, nbatch, tiles, members, w...]
where the time goes in v2:
time: 41.3 us; the launch traced here: 41.1 us
  Pallas kernels  36.9 us (89%)
  local copies, waits for them, and re-layouts  3.47 us (8%)
  between operations  0.73 us (2%)
    pallas_call x1, Pallas kernels, on_device(): pl.pallas_call(functools.partial(kernel, nbatch, members, width), out_sha...  20.6 us
    pallas_call x1, Pallas kernels, on_device(): pl.pallas_call(functools.partial(gather_kernel, nbatch, tiles, members, w...  16.4 us
    unnamed x11, local copies, waits for them, and re-layouts  1.96 us
    broadcast_in_dim x1, local copies, waits for them, and re-layouts, on_device(): return out[:, None, :]  1.51 us

profile of v2, /device:TPU:0, one launch (start us, length us, event | category | flops | bytes accessed | tf_op | source)
XLA Modules:
  0.0 41.1 jit_solution(4291201078292913841)
XLA Ops:
  0.7 0.0 copy-start
  0.7 0.0 copy-start.4
  0.7 1.3 %copy.11 = f32[80,1,2048]{2,0,1:T(8,128)S(1)} copy(f32[80,1,2048]{2,1,0:T(1,128)} %param.7) | data formatting | bytes 1310720
  2.0 0.0 copy-start.1
  2.0 0.0 copy-start.2
  2.0 0.0 copy-start.3
  2.0 0.0 copy-done
  2.0 0.0 copy-done.4
  2.0 0.6 %copy-done.1 = f32[1,1,128]{2,1,0:T(1,128)S(1)} copy-done((f32[1,1,128]{2,1,0:T(1,128)S(1)}, f32[1,1,128]{2,1,0:T(1,128)}, u32[]{:S(2)}) %copy-start.1) | copy-done | bytes 536
  2.6 0.0 copy-done.2
  2.7 0.0 copy-done.3
  2.7 16.4 %shard_map.73.obs_ref = f32[8,88,256]{2,1,0:T(8,128)S(1)} custom-call(s32[1,1]{1,0:T(1,128)S(6)} %copy.12.count_ref, f32[80,128]{1,0:T(8,128)S(1)} %bitcast.12, f32[1,128]{1,0:T(1,128)S(1)} %bitcast.13, f32[1,128]{1,0:T(1,128)S(1)} %bitcast.14, s32[1,128]{1,0:T(1,128)S(1)} %bitcast.15, s32[1,128]{1,0:T(1,128)S(1)} %bitcast.16), custom_call_target="tpu_custom_call" | custom-call | tf_op jit(solution)/shard_map/pallas_call | solution.py:203
  19.1 20.6 %shard_map.74 = f32[80,2048]{1,0:T(8,128)S(1)} custom-call(s32[1]{0:T(128)} %bitcast.scal_ref, f32[8,88,256]{2,1,0:T(8,128)S(1)} %shard_map.73.obs_ref, f32[80,2048]{1,0:T(8,128)S(1)} %bitcast.10), custom_call_target="tpu_custom_call" | custom-call | tf_op jit(solution)/shard_map/pallas_call | solution.py:225
  39.6 1.5 %copy.8 = f32[80,1,2048]{2,1,0:T(1,128)} copy(f32[80,1,2048]{2,0,1:T(8,128)S(1)} %bitcast.11) | data formatting | bytes 1310720 | tf_op jit(solution)/shard_map/broadcast_in_dim | solution.py:241
Async XLA Ops:
  0.7 1.4 %copy-start = (f32[1,80,1,128]{3,2,1,0:T(1,128)S(1)}, f32[1,80,1,128]{3,2,1,0:T(1,128)}, u32[]{:S(2)}) copy-start(f32[1,80,1,128]{3,2,1,0:T(1,128)} %param.8) | copy-start | bytes 122884
  0.7 1.4 %copy-start.4 = (s32[1,1,128]{2,1,0:T(1,128)S(1)}, s32[1,1,128]{2,1,0:T(1,128)}, u32[]{:S(2)}) copy-start(s32[1,1,128]{2,1,0:T(1,128)} %param.12) | copy-start | bytes 1540
  2.0 0.7 %copy-start.1 = (f32[1,1,128]{2,1,0:T(1,128)S(1)}, f32[1,1,128]{2,1,0:T(1,128)}, u32[]{:S(2)}) copy-start(f32[1,1,128]{2,1,0:T(1,128)} %param.9) | copy-start | bytes 1540
  2.0 0.7 %copy-start.2 = (f32[1,1,128]{2,1,0:T(1,128)S(1)}, f32[1,1,128]{2,1,0:T(1,128)}, u32[]{:S(2)}) copy-start(f32[1,1,128]{2,1,0:T(1,128)} %param.10) | copy-start | bytes 1540
  2.0 0.7 %copy-start.3 = (s32[1,1,128]{2,1,0:T(1,128)S(1)}, s32[1,1,128]{2,1,0:T(1,128)}, u32[]{:S(2)}) copy-start(s32[1,1,128]{2,1,0:T(1,128)} %param.11) | copy-start | bytes 1540

commit v3 on v2

--- a/solution.py
+++ b/solution.py
@@ -9,8 +9,8 @@
 
 EPSILON = 1e-06
 LANES = 256
-GROUP = 2
-CELL_GROUP = 4
+GROUP = 4
+CELL_GROUP = 8
 F32 = jnp.float32
 BF16 = jnp.bfloat16
 
@@ -125,7 +125,7 @@
     cell = scal_ref[0] + lax.broadcasted_iota(jnp.int32, (8, cells), 1)
     pos_ref[:, first:] = cell.astype(F32)
 
-    def step(b, carry):
+    def prepare(b):
         cols = pl.ds(pl.multiple_of(b * width, width), width)
         now = z_ref[:, cols]
         info = info_ref[b]
@@ -138,22 +138,29 @@
         factor = jnp.sqrt(post / prior) - 1.0
         increment = shift + factor * anomaly
         inc_high, inc_low = split(increment)
-        inc_ref[...] = jnp.concatenate([inc_high, inc_low], axis=0)
+        inc = jnp.concatenate([inc_high, inc_low], axis=0)
         scaled = anomaly * (1.0 / ((members - 1) * prior))
         high = scaled.astype(BF16).astype(F32)
         stacked = jnp.concatenate(
             [high, high, scaled - high, jnp.zeros((pad, width), F32)], axis=0
         )
-        lhs_ref[...] = jnp.transpose(stacked).astype(BF16)
+        lhs = jnp.transpose(stacked).astype(BF16)
         turned = jnp.transpose(jnp.concatenate([info] * (128 // info.shape[0]), axis=0))
-        pk_ref[...] = jnp.broadcast_to(turned[:, 2:3], (width, LANES))
-        wk_ref[...] = jnp.broadcast_to(turned[:, 3:4], (width, LANES))
-
-        def group(size, offset, g, inner):
+        pk = jnp.broadcast_to(turned[:, 2:3], (width, LANES))
+        wk = jnp.broadcast_to(turned[:, 3:4], (width, LANES))
+        return lhs, inc, pk, wk
+
+    def keep(terms):
+        lhs_ref[...], inc_ref[...], pk_ref[...], wk_ref[...] = terms
+
+    def step(b, carry):
+        def group(size, offset, following, g, inner):
             base = offset + g * (size * LANES)
             spans = [
                 pl.ds(pl.multiple_of(base + i * LANES, LANES), LANES) for i in range(size)
             ]
+            if following is not None:
+                terms = prepare(following)
             values = [z_ref[:, span] for span in spans]
             places = [pos_ref[0:1, span] for span in spans]
             lhs = lhs_ref[...]
@@ -173,15 +180,21 @@
                 results.append(z + (both[:members] + (both[members:] + low)))
             for span, result in zip(spans, results):
                 z_ref[:, span] = result
+            if following is not None:
+                keep(terms)
             return inner
 
         near_count = GROUP * LANES
         lax.fori_loop(((b + 1) * width) // near_count, first // near_count,
-                      functools.partial(group, GROUP, 0), 0)
-        lax.fori_loop(0, cells // (CELL_GROUP * LANES),
-                      functools.partial(group, CELL_GROUP, first), 0)
+                      functools.partial(group, GROUP, 0, None), 0)
+        bodies = cells // (CELL_GROUP * LANES)
+        if bodies > 1:
+            lax.fori_loop(0, bodies - 1,
+                          functools.partial(group, CELL_GROUP, first, None), 0)
+        group(CELL_GROUP, first, jnp.minimum(b + 1, nbatch - 1), bodies - 1, 0)
         return carry
 
+    keep(prepare(0))
     lax.fori_loop(0, nbatch, step, 0)
     out_ref[...] = z_ref[:, first:]
 

time: 41.3 us -> 38.2 us (0.925)
  Pallas kernels: 36.9 us -> 33.9 us
    pallas_call x1, Pallas kernels: 20.6 us -> 17.5 us  [on_device(): pl.pallas_call(functools.partial(kernel, nbatch, members, width), out_sha...]
where the time goes in v3:
time: 38.2 us; the launch traced here: 38.1 us
  Pallas kernels  33.9 us (89%)
  local copies, waits for them, and re-layouts  3.47 us (9%)
  between operations  0.73 us (2%)
    pallas_call x1, Pallas kernels, on_device(): pl.pallas_call(functools.partial(kernel, nbatch, members, width), out_sha...  17.5 us
    pallas_call x1, Pallas kernels, on_device(): pl.pallas_call(functools.partial(gather_kernel, nbatch, tiles, members, w...  16.4 us
    unnamed x11, local copies, waits for them, and re-layouts  1.96 us
    broadcast_in_dim x1, local copies, waits for them, and re-layouts, on_device(): return out[:, None, :]  1.51 us

profile of v3, /device:TPU:0, one launch (start us, length us, event | category | flops | bytes accessed | tf_op | source)
XLA Modules:
  0.0 38.1 jit_solution(14197698666514478776)
XLA Ops:
  0.7 0.0 copy-start
  0.7 0.0 copy-start.4
  0.7 1.3 %copy.11 = f32[80,1,2048]{2,0,1:T(8,128)S(1)} copy(f32[80,1,2048]{2,1,0:T(1,128)} %param.7) | data formatting | bytes 1310720
  2.0 0.0 copy-start.1
  2.0 0.0 copy-start.2
  2.0 0.0 copy-start.3
  2.0 0.0 copy-done
  2.0 0.0 copy-done.4
  2.0 0.6 %copy-done.1 = f32[1,1,128]{2,1,0:T(1,128)S(1)} copy-done((f32[1,1,128]{2,1,0:T(1,128)S(1)}, f32[1,1,128]{2,1,0:T(1,128)}, u32[]{:S(2)}) %copy-start.1) | copy-done | bytes 536
  2.6 0.0 copy-done.2
  2.7 0.0 copy-done.3
  2.7 16.4 %shard_map.73.obs_ref = f32[8,88,256]{2,1,0:T(8,128)S(1)} custom-call(s32[1,1]{1,0:T(1,128)S(6)} %copy.12.count_ref, f32[80,128]{1,0:T(8,128)S(1)} %bitcast.12, f32[1,128]{1,0:T(1,128)S(1)} %bitcast.13, f32[1,128]{1,0:T(1,128)S(1)} %bitcast.14, s32[1,128]{1,0:T(1,128)S(1)} %bitcast.15, s32[1,128]{1,0:T(1,128)S(1)} %bitcast.16), custom_call_target="tpu_custom_call" | custom-call | tf_op jit(solution)/shard_map/pallas_call | solution.py:216
  19.1 17.5 %shard_map.74 = f32[80,2048]{1,0:T(8,128)S(1)} custom-call(s32[1]{0:T(128)} %bitcast.scal_ref, f32[8,88,256]{2,1,0:T(8,128)S(1)} %shard_map.73.obs_ref, f32[80,2048]{1,0:T(8,128)S(1)} %bitcast.10), custom_call_target="tpu_custom_call" | custom-call | tf_op jit(solution)/shard_map/pallas_call | solution.py:238
  36.5 1.5 %copy.8 = f32[80,1,2048]{2,1,0:T(1,128)} copy(f32[80,1,2048]{2,0,1:T(8,128)S(1)} %bitcast.11) | data formatting | bytes 1310720 | tf_op jit(solution)/shard_map/broadcast_in_dim | solution.py:254
Async XLA Ops:
  0.7 1.4 %copy-start = (f32[1,80,1,128]{3,2,1,0:T(1,128)S(1)}, f32[1,80,1,128]{3,2,1,0:T(1,128)}, u32[]{:S(2)}) copy-start(f32[1,80,1,128]{3,2,1,0:T(1,128)} %param.8) | copy-start | bytes 122884
  0.7 1.4 %copy-start.4 = (s32[1,1,128]{2,1,0:T(1,128)S(1)}, s32[1,1,128]{2,1,0:T(1,128)}, u32[]{:S(2)}) copy-start(s32[1,1,128]{2,1,0:T(1,128)} %param.12) | copy-start | bytes 1540
  2.0 0.7 %copy-start.1 = (f32[1,1,128]{2,1,0:T(1,128)S(1)}, f32[1,1,128]{2,1,0:T(1,128)}, u32[]{:S(2)}) copy-start(f32[1,1,128]{2,1,0:T(1,128)} %param.9) | copy-start | bytes 1540
  2.0 0.7 %copy-start.2 = (f32[1,1,128]{2,1,0:T(1,128)S(1)}, f32[1,1,128]{2,1,0:T(1,128)}, u32[]{:S(2)}) copy-start(f32[1,1,128]{2,1,0:T(1,128)} %param.10) | copy-start | bytes 1540
  2.0 0.7 %copy-start.3 = (s32[1,1,128]{2,1,0:T(1,128)S(1)}, s32[1,1,128]{2,1,0:T(1,128)}, u32[]{:S(2)}) copy-start(s32[1,1,128]{2,1,0:T(1,128)} %param.11) | copy-start | bytes 1540

commit v4 on v3

--- a/solution.py
+++ b/solution.py
@@ -9,7 +9,7 @@
 
 EPSILON = 1e-06
 LANES = 256
-GROUP = 4
+GROUP = 2
 CELL_GROUP = 8
 F32 = jnp.float32
 BF16 = jnp.bfloat16

time: 38.2 us -> 39.6 us (1.037)
  Pallas kernels: 33.9 us -> 35.2 us
    pallas_call x1, Pallas kernels: 17.5 us -> 18.9 us  [on_device(): pl.pallas_call(functools.partial(kernel, nbatch, members, width), out_sha...]
where the time goes in v4:
time: 39.6 us; the launch traced here: 39.4 us
  Pallas kernels  35.2 us (89%)
  local copies, waits for them, and re-layouts  3.47 us (9%)
  between operations  0.73 us (2%)
    pallas_call x1, Pallas kernels, on_device(): pl.pallas_call(functools.partial(kernel, nbatch, members, width), out_sha...  18.9 us
    pallas_call x1, Pallas kernels, on_device(): pl.pallas_call(functools.partial(gather_kernel, nbatch, tiles, members, w...  16.4 us
    unnamed x11, local copies, waits for them, and re-layouts  1.96 us
    broadcast_in_dim x1, local copies, waits for them, and re-layouts, on_device(): return out[:, None, :]  1.51 us

profile of v4, /device:TPU:0, one launch (start us, length us, event | category | flops | bytes accessed | tf_op | source)
XLA Modules:
  0.0 39.4 jit_solution(14968426433084908037)
XLA Ops:
  0.7 0.0 copy-start
  0.7 0.0 copy-start.4
  0.7 1.3 %copy.11 = f32[80,1,2048]{2,0,1:T(8,128)S(1)} copy(f32[80,1,2048]{2,1,0:T(1,128)} %param.7) | data formatting | bytes 1310720
  2.0 0.0 copy-start.1
  2.0 0.0 copy-start.2
  2.0 0.0 copy-start.3
  2.0 0.0 copy-done
  2.0 0.0 copy-done.4
  2.0 0.6 %copy-done.1 = f32[1,1,128]{2,1,0:T(1,128)S(1)} copy-done((f32[1,1,128]{2,1,0:T(1,128)S(1)}, f32[1,1,128]{2,1,0:T(1,128)}, u32[]{:S(2)}) %copy-start.1) | copy-done | bytes 536
  2.6 0.0 copy-done.2
  2.7 0.0 copy-done.3
  2.7 16.4 %shard_map.73.obs_ref = f32[8,88,256]{2,1,0:T(8,128)S(1)} custom-call(s32[1,1]{1,0:T(1,128)S(6)} %copy.12.count_ref, f32[80,128]{1,0:T(8,128)S(1)} %bitcast.12, f32[1,128]{1,0:T(1,128)S(1)} %bitcast.13, f32[1,128]{1,0:T(1,128)S(1)} %bitcast.14, s32[1,128]{1,0:T(1,128)S(1)} %bitcast.15, s32[1,128]{1,0:T(1,128)S(1)} %bitcast.16), custom_call_target="tpu_custom_call" | custom-call | tf_op jit(solution)/shard_map/pallas_call | solution.py:216
  19.1 18.9 %shard_map.74 = f32[80,2048]{1,0:T(8,128)S(1)} custom-call(s32[1]{0:T(128)} %bitcast.scal_ref, f32[8,88,256]{2,1,0:T(8,128)S(1)} %shard_map.73.obs_ref, f32[80,2048]{1,0:T(8,128)S(1)} %bitcast.10), custom_call_target="tpu_custom_call" | custom-call | tf_op jit(solution)/shard_map/pallas_call | solution.py:238
  37.9 1.5 %copy.8 = f32[80,1,2048]{2,1,0:T(1,128)} copy(f32[80,1,2048]{2,0,1:T(8,128)S(1)} %bitcast.11) | data formatting | bytes 1310720 | tf_op jit(solution)/shard_map/broadcast_in_dim | solution.py:254
Async XLA Ops:
  0.7 1.4 %copy-start = (f32[1,80,1,128]{3,2,1,0:T(1,128)S(1)}, f32[1,80,1,128]{3,2,1,0:T(1,128)}, u32[]{:S(2)}) copy-start(f32[1,80,1,128]{3,2,1,0:T(1,128)} %param.8) | copy-start | bytes 122884
  0.7 1.4 %copy-start.4 = (s32[1,1,128]{2,1,0:T(1,128)S(1)}, s32[1,1,128]{2,1,0:T(1,128)}, u32[]{:S(2)}) copy-start(s32[1,1,128]{2,1,0:T(1,128)} %param.12) | copy-start | bytes 1540
  2.0 0.7 %copy-start.1 = (f32[1,1,128]{2,1,0:T(1,128)S(1)}, f32[1,1,128]{2,1,0:T(1,128)}, u32[]{:S(2)}) copy-start(f32[1,1,128]{2,1,0:T(1,128)} %param.9) | copy-start | bytes 1540
  2.0 0.7 %copy-start.2 = (f32[1,1,128]{2,1,0:T(1,128)S(1)}, f32[1,1,128]{2,1,0:T(1,128)}, u32[]{:S(2)}) copy-start(f32[1,1,128]{2,1,0:T(1,128)} %param.10) | copy-start | bytes 1540
  2.0 0.7 %copy-start.3 = (s32[1,1,128]{2,1,0:T(1,128)S(1)}, s32[1,1,128]{2,1,0:T(1,128)}, u32[]{:S(2)}) copy-start(s32[1,1,128]{2,1,0:T(1,128)} %param.11) | copy-start | bytes 1540
